TPU v7x, 32 devices: a whole 2x2x4 slice. The times are simulated.
32 devices in a mesh: node: 4 (over y, x), replica: 8 (over z, core).
Axes of the slice: x: 2, y: 2, z: 4, core: 2. Of those that a mesh axis runs over, the one named last changes fastest.
Arguments:
- hidden: bfloat16 [8192, 4096], P(('node', 'replica')), may hold values from -12 to 12
- cotangent: bfloat16 [8192, 2560], P(('node', 'replica')), may hold values from -0.125 to 0.125
- scales: float32 [4096, 20], P('node'), may hold values from 0.04 to 0.8
Outputs:
- weight_grad: float32 [4096, 2560], P(('node', 'replica'))
All inputs are finite; a program needn't handle non-finite values.
Results may differ from a plain program's by a relative error of at most 0.017.
Values may be sent and summed in bfloat16 or wider, within the bound.
A program may use at most 128 MiB of HBM per device.

v0:
```python
import math

import jax
import jax.numpy as jnp
from jax import lax
from jax.sharding import PartitionSpec as P


def hadamard_table():
    index_row = jnp.arange(128, dtype=jnp.int32)[:, None]
    index_col = jnp.arange(128, dtype=jnp.int32)[None, :]
    common = jnp.bitwise_and(index_row, index_col)
    parity = jnp.zeros((128, 128), jnp.int32)
    for bit_index in range(7):
        parity = parity + jnp.bitwise_and(jnp.right_shift(common, bit_index), 1)
    sign_table = 1.0 - 2.0 * jnp.bitwise_and(parity, 1).astype(jnp.float32)
    return sign_table / jnp.float32(math.sqrt(128.0))


def rotate(matrix, table):
    row_count, width = matrix.shape
    blocks = matrix.reshape(row_count, width // 128, 128)
    turned = jnp.einsum("rbk,kj->rbj", blocks, table, precision=lax.Precision.HIGHEST)
    return turned.reshape(row_count, width)


def on_device(hidden, cotangent, scales):
    table = hadamard_table()
    width = cotangent.shape[1]
    node_sum = lax.psum_scatter(
        lax.dot_general(
            hidden, cotangent, (((0,), (0,)), ((), ())), preferred_element_type=jnp.float32
        ).astype(jnp.bfloat16),
        "node",
        scatter_dimension=0,
        tiled=True,
    ).astype(jnp.float32)
    rotated = rotate(node_sum, table)
    expanded = jnp.repeat(scales, 128, axis=1)
    levels = jnp.clip(rotated / expanded, -7.0, 7.0).astype(jnp.bfloat16)
    arrived = lax.all_to_all(levels, "replica", split_axis=0, concat_axis=1, tiled=True)
    replicas = lax.axis_size("replica")
    final_rows = levels.shape[0] // replicas
    summed = jnp.sum(arrived.reshape(final_rows, replicas, width).astype(jnp.float32), axis=1)
    own_scales = lax.dynamic_slice_in_dim(
        expanded, lax.axis_index("replica") * final_rows, final_rows, 0
    )
    return rotate(summed * own_scales, table)


def solution(mesh):
    in_specs = (P(("node", "replica"), None), P(("node", "replica"), None), P("node", None))
    out_specs = P(("node", "replica"), None)
    return jax.shard_map(
        on_device, mesh=mesh, in_specs=in_specs, out_specs=out_specs, check_vma=False
    )
```

profile of v0, /device:TPU:0, one launch (start us, length us, event | category | flops | bytes accessed | tf_op | source)
XLA Modules:
  0.0 378.5 jit_solution(2807400503725992986)
XLA Ops:
  6.5 0.0 copy-start
  6.5 0.0 reduce-scatter.2.cloned.1.call-start
  6.5 1.6 copy-done
  8.1 11.2 %convolution_convert_fusion = bf16[4096,2560]{1,0:T(8,128)(2,1)} fusion(bf16[256,4096]{1,0:T(8,128)(2,1)S(1)} %copy-done, bf16[256,2560]{1,0:T(8,128)(2,1)} %param.4), kind=kOutput, calls=%fused_computation | convolution fusion | flops 5379194880 | bytes 24379392 | tf_op jit(solution)/shard_map/dot_general | solution.py:31
  19.3 0.0 reduce-scatter.2.cloned.1.call-update
  19.4 0.0 copy-start.2
  19.4 190.6 %reduce-scatter.2.cloned.1.call-done = bf16[1024,2560]{1,0:T(8,128)(2,1)} async-done(((bf16[4096,2560]{1,0:T(8,128)(2,1)}), bf16[1024,2560]{1,0:T(8,128)(2,1)}) %reduce-scatter.2.cloned.1.call-update) | async-done | bytes 5242896 | tf_op jit(solution)/shard_map/reduce_scatter | solution.py:30
  210.0 8.0 %copy.14 = bf16[1024,2560]{0,1:T(8,128)(2,1)} copy(bf16[1024,2560]{1,0:T(8,128)(2,1)} %reduce-scatter.2.cloned.1.call-done) | data formatting | bytes 10485760 | tf_op jit(solution)/shard_map/reduce_scatter | solution.py:30
  218.0 0.0 copy-done.2
  218.0 9.7 %clamp_convert_fusion = bf16[1024,20,128]{2,0,1:T(8,128)(2,1)} fusion(f32[1024,20]{0,1:T(8,128)S(1)} %copy-done.2, bf16[1024,20,128]{0,2,1:T(8,128)(2,1)} %bitcast.22), kind=kOutput, calls=%fused_computation.2 | convolution fusion | flops 4034822144 | bytes 10567680 | tf_op jit(solution)/shard_map/rbk,kj->rbj/dot_general | solution.py:23
  227.7 7.9 %copy.17 = bf16[1024,20,128]{0,2,1:T(8,128)(2,1)} copy(bf16[1024,20,128]{2,0,1:T(8,128)(2,1)} %clamp_convert_fusion) | data formatting | bytes 10485760 | tf_op jit(solution)/shard_map/convert_element_type | solution.py:40
  235.7 3.8 %copy.27 = bf16[320,8,8,128]{3,2,1,0:T(8,128)(2,1)S(1)} copy(bf16[320,8,8,128]{3,1,2,0:T(8,128)(2,1)} %bitcast.19) | data formatting | bytes 10485760
  239.5 3.2 copy.18
  242.7 4.6 %all-to-all-start = ((bf16[8,128,2560]{1,2,0:T(8,128)(2,1)}), bf16[8,128,2560]{1,2,0:T(8,128)(2,1)}, u32[]{:S(2)}, u32[]{:S(2)}) async-start(bf16[8,128,2560]{1,2,0:T(8,128)(2,1)} %copy.18), calls=%async_computation.1 | async-start | bytes 10485760 | tf_op jit(solution)/shard_map/all_to_all | solution.py:41
  247.4 116.5 %all-to-all-done = bf16[8,128,2560]{1,2,0:T(8,128)(2,1)} async-done(((bf16[8,128,2560]{1,2,0:T(8,128)(2,1)}), bf16[8,128,2560]{1,2,0:T(8,128)(2,1)}, u32[]{:S(2)}, u32[]{:S(2)}) %all-to-all-start) | async-done | bytes 5242912 | tf_op jit(solution)/shard_map/all_to_all | solution.py:41
  363.9 3.3 convert_reduce_fusion
  367.2 0.0 copy-start.1
  367.3 1.3 broadcast_in_dim.2.clone
  368.6 0.2 dynamic-slice_multiply_fusion
  368.8 1.3 fusion
  370.2 1.5 copy.21
  371.6 0.0 copy-done.1
Async XLA Ops:
  6.5 1.6 copy-start
  6.5 203.5 %reduce-scatter.2.cloned.1.call-start = ((), (), s32[]{:S(2)}) async-start(), calls=%async_computation.2 | async-start | bytes 26214400 | tf_op jit(solution)/shard_map/reduce_scatter | solution.py:30
  19.4 198.6 %copy-start.2 = (f32[1024,20]{0,1:T(8,128)S(1)}, f32[1024,20]{0,1:T(8,128)}, u32[]{:S(2)}) copy-start(f32[1024,20]{0,1:T(8,128)} %param.5) | copy-start | bytes 245764
  242.7 121.2 %all-to-all-start = ((bf16[8,128,2560]{1,2,0:T(8,128)(2,1)}), bf16[8,128,2560]{1,2,0:T(8,128)(2,1)}, u32[]{:S(2)}, u32[]{:S(2)}) async-start(bf16[8,128,2560]{1,2,0:T(8,128)(2,1)} %copy.18), calls=%async_computation.1 | async-start | bytes 10485760 | tf_op jit(solution)/shard_map/all_to_all | solution.py:41
  367.2 4.4 %copy-start.1 = (bf16[256,4096]{1,0:T(8,128)(2,1)S(1)}, bf16[256,4096]{1,0:T(8,128)(2,1)}, u32[]{:S(2)}) copy-start(bf16[256,4096]{1,0:T(8,128)(2,1)} %param.3) | copy-start | bytes 6291460
Sparse Core Ops, SparseCore 0:
  19.5 190.4 reduce-scatter.1
where the time goes:
time: 379 us; the launch traced here: 378 us
  waiting for transfers between devices  307 us (81%)
  local copies, waits for them, and re-layouts  27.3 us (7%)
  matrix products  22.3 us (6%)
  between operations  13.5 us (4%)
  starting transfers between devices  4.65 us (1%)
    reduce_scatter x1, waiting for transfers between devices, on_device(): lax.psum_scatter(lax.dot_general(hidden, cotangent, (((0,), (0,)), ((), (...  191 us
    all_to_all x1, waiting for transfers between devices, on_device(): lax.all_to_all(levels, 'replica', split_axis=0, concat_axis=1, tiled=True)  117 us
    dot_general x1, matrix products, on_device(): lax.dot_general(hidden, cotangent, (((0,), (0,)), ((), ())), preferred_el...  11.2 us
    convert_element_type x2, local copies, waits for them, and re-layouts, on_device(): levels = jnp.clip(rotated / expanded, -7.0, 7.0).astype(jnp.bfloat16)  11.1 us
    dot_general x2, matrix products, rotate(): jnp.einsum('rbk,kj->rbj', blocks, table, precision=lax.Precision.HIGHEST)  11.1 us
    reduce_scatter x1, local copies, waits for them, and re-layouts, on_device(): lax.psum_scatter(lax.dot_general(hidden, cotangent, (((0,), (0,)), ((), (...  7.97 us
  transfers between devices with their start and end apart: 2, of which 2 were waited for; matrix products, arithmetic and copies ran while one was open for 0% of the time, Pallas kernels for 0%

commit v1 on v0

v1 whole, which is shorter than its diff:
```python
import functools
import math

import jax
import jax.numpy as jnp
from jax import lax
from jax.experimental import pallas as pl
from jax.experimental.pallas import tpu as pltpu
from jax.sharding import PartitionSpec as P

MESH = pl.DeviceIdType.MESH
BLOCK = 128
WINDOW = 3


def kernel(
    nodes, replicas, chunk,
    hidden, cotangent, scales, out,
    hid, hid_t, cot, table, inverse, forward, levels, partner_in, pair, arrived,
    local_sem, hid_send, hid_recv, cot_send, cot_recv, pair_send, pair_recv, z_send, z_recv,
):
    chips = replicas // 2
    tokens, slab = hidden.shape
    width = cotangent.shape[1]
    chunks = width // chunk
    rows = slab // nodes
    final = rows // replicas
    tile = 2 * final
    scale_cols = scales.shape[1]
    node = lax.axis_index("node")
    replica = lax.axis_index("replica")
    chip = replica // 2
    core = lax.rem(replica, 2)
    partner = chip * 2 + (1 - core)

    def peer_node(step):
        return lax.rem(node + step, nodes)

    def peer_replica(step):
        return lax.rem(chip + step, chips) * 2 + core

    barrier = pltpu.get_barrier_semaphore()
    for step in range(1, nodes):
        pl.semaphore_signal(barrier, inc=1, device_id={"node": peer_node(step)}, device_id_type=MESH)
    pl.semaphore_signal(barrier, inc=1, device_id={"replica": partner}, device_id_type=MESH)
    for step in range(1, chips):
        pl.semaphore_signal(barrier, inc=1, device_id={"replica": peer_replica(step)}, device_id_type=MESH)

    def own_hidden():
        begin = pl.multiple_of(node * rows, BLOCK)
        return pltpu.make_async_copy(hidden.at[:, pl.ds(begin, rows)], hid.at[0], local_sem.at[0])

    def own_cot(j):
        begin = pl.multiple_of(j * chunk, BLOCK)
        return pltpu.make_async_copy(cotangent.at[:, pl.ds(begin, chunk)], cot.at[j, 0], local_sem.at[1 + j])

    def hid_copy(step):
        to = peer_node(step)
        begin = pl.multiple_of(to * rows, BLOCK)
        return pltpu.make_async_remote_copy(
            hidden.at[:, pl.ds(begin, rows)], hid.at[step], hid_send.at[step - 1], hid_recv.at[step - 1],
            device_id={"node": to}, device_id_type=MESH,
        )

    def cot_copy(j, step):
        begin = pl.multiple_of(j * chunk, BLOCK)
        return pltpu.make_async_remote_copy(
            cotangent.at[:, pl.ds(begin, chunk)], cot.at[j, step],
            cot_send.at[j, step - 1], cot_recv.at[j, step - 1],
            device_id={"node": peer_node(step)}, device_id_type=MESH,
        )

    def pair_copy(j):
        return pltpu.make_async_remote_copy(
            levels.at[j, 1 - core], partner_in.at[j], pair_send.at[j], pair_recv.at[j],
            device_id={"replica": partner}, device_id_type=MESH,
        )

    def z_copy(j, step):
        to = lax.rem(chip + step, chips)
        return pltpu.make_async_remote_copy(
            pair.at[j, to], arrived.at[j, step - 1], z_send.at[j, step - 1], z_recv.at[j, step - 1],
            device_id={"replica": to * 2 + core}, device_id_type=MESH,
        )

    own_hidden().start()

    @pl.loop(0, chunks)
    def _(j):
        own_cot(j).start()

    pl.semaphore_wait(barrier, nodes - 1 + chips)
    for step in range(1, nodes):
        hid_copy(step).start()
    for j in range(min(WINDOW, chunks)):
        for step in range(1, nodes):
            cot_copy(j, step).start()

    row_index = lax.broadcasted_iota(jnp.int32, (chunk, chunk), 0)
    col_index = lax.broadcasted_iota(jnp.int32, (chunk, chunk), 1)
    bits = jnp.bitwise_and(jnp.bitwise_and(row_index, col_index), BLOCK - 1)
    for shift in (4, 2, 1):
        bits = jnp.bitwise_xor(bits, jnp.right_shift(bits, shift))
    signs = 1.0 - 2.0 * jnp.bitwise_and(bits, 1).astype(jnp.float32)
    same = jnp.right_shift(row_index, 7) == jnp.right_shift(col_index, 7)
    table[...] = jnp.where(same, signs, 0.0).astype(jnp.bfloat16)

    def split_store(ref, value):
        high = value.astype(jnp.bfloat16)
        low = (value - high.astype(jnp.float32)).astype(jnp.bfloat16)
        ref[...] = jnp.zeros_like(ref)
        ref[:, :scale_cols] = high
        ref[:, BLOCK:BLOCK + scale_cols] = low

    norm = 1.0 / math.sqrt(BLOCK)
    split_store(inverse, norm / scales[...])
    split_store(forward, norm * scales[...])

    def spread(j):
        source = lax.broadcasted_iota(jnp.int32, (2 * BLOCK, chunk), 0)
        target = lax.broadcasted_iota(jnp.int32, (2 * BLOCK, chunk), 1)
        hit = jnp.bitwise_and(source, BLOCK - 1) == jnp.right_shift(target, 7) + j * (chunk // BLOCK)
        return jnp.where(hit, 1.0, 0.0).astype(jnp.bfloat16)

    def mul(left, right):
        return jnp.dot(left, right, preferred_element_type=jnp.float32)

    def rotate(value):
        high = value.astype(jnp.bfloat16)
        low = (value - high.astype(jnp.float32)).astype(jnp.bfloat16)
        return mul(high, table[...]) + mul(low, table[...])

    for step in range(nodes):
        if step == 0:
            own_hidden().wait()
        else:
            hid_copy(step).wait_recv()
        for part in range(rows // BLOCK):
            span = slice(part * BLOCK, (part + 1) * BLOCK)
            hid_t[step, span, :] = hid[step, :, span].T

    @pl.loop(0, chunks)
    def _(j):
        @pl.when(j + WINDOW < chunks)
        def _():
            for step in range(1, nodes):
                cot_copy(j + WINDOW, step).start()

        own_cot(j).wait()
        for step in range(1, nodes):
            cot_copy(j, step).wait_recv()
        expand = spread(j)

        @pl.loop(0, chips)
        def _(z):
            span = pl.ds(pl.multiple_of(z * tile, tile), tile)
            total = None
            for step in range(nodes):
                term = mul(hid_t[step, span, :], cot[j, step]).astype(jnp.bfloat16).astype(jnp.float32)
                total = term if total is None else total + term
            level = rotate(total) * mul(inverse[span, :], expand)
            level = jnp.clip(level, -7.0, 7.0).astype(jnp.bfloat16)
            levels[j, 0, z] = level[:final]
            levels[j, 1, z] = level[final:]

        pair_copy(j).start()
        pair_copy(j).wait_recv()

        @pl.loop(0, chips)
        def _(z):
            both = levels[j, core, z].astype(jnp.float32) + partner_in[j, z].astype(jnp.float32)
            pair[j, z] = both.astype(jnp.bfloat16)

        for step in range(1, chips):
            z_copy(j, step).start()

    own_rows = pl.ds(pl.multiple_of(replica * final, final), final)

    @pl.loop(0, chunks)
    def _(j):
        total = pair[j, chip].astype(jnp.float32)
        for step in range(1, chips):
            z_copy(j, step).wait_recv()
            total = total + arrived[j, step - 1].astype(jnp.float32)
        total = total * mul(forward[own_rows, :], spread(j))
        out[:, pl.ds(pl.multiple_of(j * chunk, BLOCK), chunk)] = rotate(total)

    for step in range(1, nodes):
        hid_copy(step).wait_send()

    @pl.loop(0, chunks)
    def _(j):
        for step in range(1, nodes):
            cot_copy(j, step).wait_send()
        pair_copy(j).wait_send()
        for step in range(1, chips):
            z_copy(j, step).wait_send()


def on_device(nodes, replicas, hidden, cotangent, scales):
    tokens, slab = hidden.shape
    width = cotangent.shape[1]
    chunk = 2 * BLOCK
    chunks = width // chunk
    rows = slab // nodes
    final = rows // replicas
    chips = replicas // 2
    bf16 = jnp.bfloat16
    dma = pltpu.SemaphoreType.DMA
    return pl.pallas_call(
        functools.partial(kernel, nodes, replicas, chunk),
        out_shape=jax.ShapeDtypeStruct((final, width), jnp.float32),
        in_specs=[
            pl.BlockSpec(memory_space=pl.ANY),
            pl.BlockSpec(memory_space=pl.ANY),
            pl.BlockSpec(memory_space=pltpu.VMEM),
        ],
        out_specs=pl.BlockSpec(memory_space=pltpu.VMEM),
        scratch_shapes=[
            pltpu.VMEM((nodes, tokens, rows), bf16),
            pltpu.VMEM((nodes, rows, tokens), bf16),
            pltpu.VMEM((chunks, nodes, tokens, chunk), bf16),
            pltpu.VMEM((chunk, chunk), bf16),
            pltpu.VMEM((rows, 2 * BLOCK), bf16),
            pltpu.VMEM((rows, 2 * BLOCK), bf16),
            pltpu.VMEM((chunks, 2, chips, final, chunk), bf16),
            pltpu.VMEM((chunks, chips, final, chunk), bf16),
            pltpu.VMEM((chunks, chips, final, chunk), bf16),
            pltpu.VMEM((chunks, chips - 1, final, chunk), bf16),
            dma((1 + chunks,)),
            dma((nodes - 1,)),
            dma((nodes - 1,)),
            dma((chunks, nodes - 1)),
            dma((chunks, nodes - 1)),
            dma((chunks,)),
            dma((chunks,)),
            dma((chunks, chips - 1)),
            dma((chunks, chips - 1)),
        ],
        compiler_params=pltpu.CompilerParams(
            collective_id=0, has_side_effects=True, vmem_limit_bytes=52 * 1024 * 1024
        ),
        cost_estimate=pl.CostEstimate(
            flops=2 * tokens * slab * width, bytes_accessed=2 * tokens * (slab + width), transcendentals=0
        ),
    )(hidden, cotangent, scales)


def solution(mesh):
    in_specs = (P(("node", "replica"), None), P(("node", "replica"), None), P("node", None))
    out_specs = P(("node", "replica"), None)
    return jax.shard_map(
        functools.partial(on_device, mesh.shape["node"], mesh.shape["replica"]),
        mesh=mesh, in_specs=in_specs, out_specs=out_specs, check_vma=False,
    )
```

time: 379 us -> 101 us (0.27)
  waiting for transfers between devices: 307 us -> 0 us
  Pallas kernels: 0 us -> 98.5 us
  local copies, waits for them, and re-layouts: 27.3 us -> 2.16 us
  matrix products: 22.3 us -> 0 us
  between operations: 13.5 us -> 0.02 us
  starting transfers between devices: 4.65 us -> 0 us
    reduce_scatter x1 -> x0, waiting for transfers between devices: 191 us -> none  [on_device(): lax.psum_scatter(lax.dot_general(hidden, cotangent, (((0,), (0,)), ((), (...]
    all_to_all x1 -> x0, waiting for transfers between devices: 117 us -> none  [on_device(): lax.all_to_all(levels, 'replica', split_axis=0, concat_axis=1, tiled=True)]
    pallas_call x0 -> x1, Pallas kernels: none -> 98.5 us  [on_device(): pl.pallas_call(functools.partial(kernel, nodes, replicas, chunk), out_sha...]
    dot_general x3 -> x0, matrix products: 22.3 us -> none  [the longest x1 11.2 us: on_device(): lax.dot_general(hidden, cotangent, (((0,), (0,)), ((), ())), preferred_el...]
    convert_element_type x2 -> x0, local copies, waits for them, and re-layouts: 11.1 us -> none  [on_device(): levels = jnp.clip(rotated / expanded, -7.0, 7.0).astype(jnp.bfloat16)]
    reduce_scatter x1 -> x0, local copies, waits for them, and re-layouts: 7.97 us -> none  [on_device(): lax.psum_scatter(lax.dot_general(hidden, cotangent, (((0,), (0,)), ((), (...]
    all_to_all x1 -> x0, starting transfers between devices: 4.65 us -> none  [on_device(): lax.all_to_all(levels, 'replica', split_axis=0, concat_axis=1, tiled=True)]
  transfers between devices with their start and end apart: 2 -> 0, of which waited for: 2 -> 0; matrix products, arithmetic and copies ran while one was open for 0% -> 0% of each run, Pallas kernels for 0% -> 0%
where the time goes in v1:
time: 101 us
  Pallas kernels  98.5 us (98%)
  local copies, waits for them, and re-layouts  2.16 us (2%)
    pallas_call x1, Pallas kernels, on_device(): pl.pallas_call(functools.partial(kernel, nodes, replicas, chunk), out_sha...  98.5 us
    unnamed x2, local copies, waits for them, and re-layouts  2.16 us

profile of v1, /device:TPU:0, one launch (start us, length us, event | category | flops | bytes accessed | tf_op | source)
XLA Modules:
  0.0 100.6 jit_solution(8708572380338088481)
XLA Ops:
  0.0 1.1 %copy.4.scales = f32[1024,20]{1,0:T(8,128)S(1)} copy(f32[1024,20]{0,1:T(8,128)} %param.5) | data formatting | bytes 163840 | tf_op args[2]
  1.1 98.5 %shard_map.37 = f32[128,2560]{1,0:T(8,128)S(1)} custom-call(bf16[256,4096]{1,0:T(8,128)(2,1)} %hidden.1, bf16[256,2560]{1,0:T(8,128)(2,1)} %cotangent.1, f32[1024,20]{1,0:T(8,128)S(1)} %copy.4.scales), custom_call_target="tpu_custom_call" | custom-call | flops 5368709120 | bytes 3407872 | tf_op jit(solution)/shard_map/pallas_call | solution.py:210
  99.6 1.1 %copy.6 = f32[128,2560]{1,0:T(8,128)} copy(f32[128,2560]{1,0:T(8,128)S(1)} %shard_map.37) | data formatting | bytes 2621440

commit v2 on v1

--- a/solution.py
+++ b/solution.py
@@ -10,14 +10,18 @@
 
 MESH = pl.DeviceIdType.MESH
 BLOCK = 128
-WINDOW = 3
+WINDOW = 4
+AHEAD = 2
+RELAY_LAG = 2
+FINISH_LAG = 4
 
 
 def kernel(
     nodes, replicas, chunk,
     hidden, cotangent, scales, out,
-    hid, hid_t, cot, table, inverse, forward, levels, partner_in, pair, arrived,
+    hid, hid_t, cot, table, inverse, forward, levels, partner_in, pair, arrived, relay_in, merged,
     local_sem, hid_send, hid_recv, cot_send, cot_recv, pair_send, pair_recv, z_send, z_recv,
+    forward_send, forward_recv, relay_send, relay_recv, cross_send, cross_recv,
 ):
     chips = replicas // 2
     tokens, slab = hidden.shape
@@ -33,7 +37,22 @@
     core = lax.rem(replica, 2)
     partner = chip * 2 + (1 - core)
 
+    square = nodes == 4
+    line = chips == 4
+    node_y, node_x = node // 2, lax.rem(node, 2)
+    side = chip // 2
+    mate = side * 2 + (1 - lax.rem(chip, 2))
+    far = 2 * (1 - side)
+    inner = lax.rem(chip, 2) == 1 - side
+    edge = lax.rem(chip, 2) == side
+    direct = (1, 2) if square else tuple(range(1, nodes))
+    halves = ((far, 2), (2 * side, 2)) if line else ((0, chips),)
+
     def peer_node(step):
+        if square:
+            across_x = 1 - node_x if step % 2 else node_x
+            across_y = 1 - node_y if step // 2 else node_y
+            return across_y * 2 + across_x
         return lax.rem(node + step, nodes)
 
     def peer_replica(step):
@@ -70,11 +89,52 @@
             device_id={"node": peer_node(step)}, device_id_type=MESH,
         )
 
-    def pair_copy(j):
-        return pltpu.make_async_remote_copy(
-            levels.at[j, 1 - core], partner_in.at[j], pair_send.at[j], pair_recv.at[j],
+    def forward_copy(j, way):
+        span = slice(way * (tokens // 2), (way + 1) * (tokens // 2))
+        return pltpu.make_async_remote_copy(
+            cot.at[j, 1 + way, span], cot.at[j, 3, span], forward_send.at[j, way], forward_recv.at[j, way],
+            device_id={"node": peer_node(2 - way)}, device_id_type=MESH,
+        )
+
+    def pass_on(j):
+        for way in range(2):
+            cot_copy(j, 1 + way).wait_recv()
+            forward_copy(j, way).start()
+
+    def pair_copy(j, half):
+        first, count = halves[half]
+        return pltpu.make_async_remote_copy(
+            levels.at[j, 1 - core, pl.ds(first, count)], partner_in.at[j, pl.ds(first, count)],
+            pair_send.at[j, half], pair_recv.at[j, half],
             device_id={"replica": partner}, device_id_type=MESH,
         )
+
+    def mate_copy(j):
+        return pltpu.make_async_remote_copy(
+            pair.at[j, mate], arrived.at[j, 0], z_send.at[j, 0], z_recv.at[j, 0],
+            device_id={"replica": mate * 2 + core}, device_id_type=MESH,
+        )
+
+    def relay_copy(j):
+        return pltpu.make_async_remote_copy(
+            pair.at[j, pl.ds(far, 2)], relay_in.at[j], relay_send.at[j], relay_recv.at[j],
+            device_id={"replica": mate * 2 + core}, device_id_type=MESH,
+        )
+
+    def cross_copy(j, k):
+        return pltpu.make_async_remote_copy(
+            merged.at[j, k], arrived.at[j, 1], cross_send.at[j, k], cross_recv.at[j],
+            device_id={"replica": (far + k) * 2 + core}, device_id_type=MESH,
+        )
+
+    def relay(j):
+        @pl.when(inner)
+        def _():
+            relay_copy(j).wait_recv()
+            for k in range(2):
+                both = pair[j, far + k].astype(jnp.float32) + relay_in[j, k].astype(jnp.float32)
+                merged[j, k] = both.astype(jnp.bfloat16)
+                cross_copy(j, k).start()
 
     def z_copy(j, step):
         to = lax.rem(chip + step, chips)
@@ -92,9 +152,13 @@
     pl.semaphore_wait(barrier, nodes - 1 + chips)
     for step in range(1, nodes):
         hid_copy(step).start()
-    for j in range(min(WINDOW, chunks)):
-        for step in range(1, nodes):
+
+    def send_cot(j):
+        for step in direct:
             cot_copy(j, step).start()
+
+    for j in range(AHEAD):
+        send_cot(j)
 
     row_index = lax.broadcasted_iota(jnp.int32, (chunk, chunk), 0)
     col_index = lax.broadcasted_iota(jnp.int32, (chunk, chunk), 1)
@@ -135,66 +199,125 @@
             own_hidden().wait()
         else:
             hid_copy(step).wait_recv()
+        if step == 1:
+            for j in range(AHEAD, WINDOW):
+                send_cot(j)
         for part in range(rows // BLOCK):
             span = slice(part * BLOCK, (part + 1) * BLOCK)
             hid_t[step, span, :] = hid[step, :, span].T
+        if square and step >= nodes - AHEAD:
+            pass_on(step - (nodes - AHEAD))
+
+    own_rows = pl.ds(pl.multiple_of(replica * final, final), final)
+
+    def finish(j):
+        total = pair[j, chip].astype(jnp.float32)
+        if line:
+            mate_copy(j).wait_recv()
+            cross_copy(j, 0).wait_recv()
+        for slot in range(arrived.shape[1]):
+            if not line:
+                z_copy(j, slot + 1).wait_recv()
+            total = total + arrived[j, slot].astype(jnp.float32)
+        total = total * mul(forward[own_rows, :], spread(j))
+        out[:, pl.ds(pl.multiple_of(j * chunk, BLOCK), chunk)] = rotate(total)
 
     @pl.loop(0, chunks)
     def _(j):
         @pl.when(j + WINDOW < chunks)
         def _():
-            for step in range(1, nodes):
-                cot_copy(j + WINDOW, step).start()
+            send_cot(j + WINDOW)
 
         own_cot(j).wait()
-        for step in range(1, nodes):
-            cot_copy(j, step).wait_recv()
+        if square:
+            @pl.when(j + AHEAD < chunks)
+            def _():
+                pass_on(j + AHEAD)
+
+            for way in range(2):
+                forward_copy(j, way).wait_recv()
+        else:
+            for step in direct:
+                cot_copy(j, step).wait_recv()
         expand = spread(j)
 
-        @pl.loop(0, chips)
-        def _(z):
-            span = pl.ds(pl.multiple_of(z * tile, tile), tile)
-            total = None
-            for step in range(nodes):
-                term = mul(hid_t[step, span, :], cot[j, step]).astype(jnp.bfloat16).astype(jnp.float32)
-                total = term if total is None else total + term
-            level = rotate(total) * mul(inverse[span, :], expand)
-            level = jnp.clip(level, -7.0, 7.0).astype(jnp.bfloat16)
-            levels[j, 0, z] = level[:final]
-            levels[j, 1, z] = level[final:]
-
-        pair_copy(j).start()
-        pair_copy(j).wait_recv()
-
-        @pl.loop(0, chips)
-        def _(z):
-            both = levels[j, core, z].astype(jnp.float32) + partner_in[j, z].astype(jnp.float32)
-            pair[j, z] = both.astype(jnp.bfloat16)
-
-        for step in range(1, chips):
-            z_copy(j, step).start()
-
-    own_rows = pl.ds(pl.multiple_of(replica * final, final), final)
+        for half, (first, count) in enumerate(halves):
+            @pl.loop(first, first + count)
+            def _(z):
+                span = pl.ds(pl.multiple_of(z * tile, tile), tile)
+                total = None
+                for step in range(nodes):
+                    term = mul(hid_t[step, span, :], cot[j, step]).astype(jnp.bfloat16).astype(jnp.float32)
+                    total = term if total is None else total + term
+                level = rotate(total) * mul(inverse[span, :], expand)
+                level = jnp.clip(level, -7.0, 7.0).astype(jnp.bfloat16)
+                levels[j, 0, z] = level[:final]
+                levels[j, 1, z] = level[final:]
+
+            pair_copy(j, half).start()
+
+        for half, (first, count) in enumerate(halves):
+            pair_copy(j, half).wait_recv()
+
+            @pl.loop(first, first + count)
+            def _(z):
+                both = levels[j, core, z].astype(jnp.float32) + partner_in[j, z].astype(jnp.float32)
+                pair[j, z] = both.astype(jnp.bfloat16)
+
+            if line and half == 0:
+                @pl.when(edge)
+                def _():
+                    relay_copy(j).start()
+
+        if line:
+            mate_copy(j).start()
+
+            @pl.when(j >= RELAY_LAG)
+            def _():
+                relay(j - RELAY_LAG)
+        else:
+            for step in range(1, chips):
+                z_copy(j, step).start()
+
+        @pl.when(j >= FINISH_LAG)
+        def _():
+            finish(j - FINISH_LAG)
+
+    if line:
+        @pl.loop(chunks - RELAY_LAG, chunks)
+        def _(j):
+            relay(j)
+
+    @pl.loop(chunks - FINISH_LAG, chunks)
+    def _(j):
+        finish(j)
+
+    for step in range(1, nodes):
+        hid_copy(step).wait_send()
 
     @pl.loop(0, chunks)
     def _(j):
-        total = pair[j, chip].astype(jnp.float32)
-        for step in range(1, chips):
-            z_copy(j, step).wait_recv()
-            total = total + arrived[j, step - 1].astype(jnp.float32)
-        total = total * mul(forward[own_rows, :], spread(j))
-        out[:, pl.ds(pl.multiple_of(j * chunk, BLOCK), chunk)] = rotate(total)
-
-    for step in range(1, nodes):
-        hid_copy(step).wait_send()
-
-    @pl.loop(0, chunks)
-    def _(j):
-        for step in range(1, nodes):
+        for step in direct:
             cot_copy(j, step).wait_send()
-        pair_copy(j).wait_send()
-        for step in range(1, chips):
-            z_copy(j, step).wait_send()
+        if square:
+            for way in range(2):
+                forward_copy(j, way).wait_send()
+        for half in range(len(halves)):
+            pair_copy(j, half).wait_send()
+        if line:
+            mate_copy(j).wait_send()
+
+            @pl.when(edge)
+            def _():
+                relay_copy(j).wait_send()
+
+            @pl.when(inner)
+            def _():
+                for k in range(2):
+                    cross_copy(j, k).wait_send()
+        else:
+            for step in range(1, chips):
+                z_copy(j, step).wait_send()
 
 
 def on_device(nodes, replicas, hidden, cotangent, scales):
@@ -205,6 +328,7 @@
     rows = slab // nodes
     final = rows // replicas
     chips = replicas // 2
+    slots = 2 if chips == 4 else chips - 1
     bf16 = jnp.bfloat16
     dma = pltpu.SemaphoreType.DMA
     return pl.pallas_call(
@@ -226,16 +350,24 @@
             pltpu.VMEM((chunks, 2, chips, final, chunk), bf16),
             pltpu.VMEM((chunks, chips, final, chunk), bf16),
             pltpu.VMEM((chunks, chips, final, chunk), bf16),
-            pltpu.VMEM((chunks, chips - 1, final, chunk), bf16),
+            pltpu.VMEM((chunks, slots, final, chunk), bf16),
+            pltpu.VMEM((chunks, 2, final, chunk), bf16),
+            pltpu.VMEM((chunks, 2, final, chunk), bf16),
             dma((1 + chunks,)),
             dma((nodes - 1,)),
             dma((nodes - 1,)),
             dma((chunks, nodes - 1)),
             dma((chunks, nodes - 1)),
+            dma((chunks, 2)),
+            dma((chunks, 2)),
+            dma((chunks, slots)),
+            dma((chunks, slots)),
+            dma((chunks, 2)),
+            dma((chunks, 2)),
             dma((chunks,)),
             dma((chunks,)),
-            dma((chunks, chips - 1)),
-            dma((chunks, chips - 1)),
+            dma((chunks, 2)),
+            dma((chunks,)),
         ],
         compiler_params=pltpu.CompilerParams(
             collective_id=0, has_side_effects=True, vmem_limit_bytes=52 * 1024 * 1024

time: 101 us -> 97.5 us (0.965)
  Pallas kernels: 98.5 us -> 95.1 us
    pallas_call x1, Pallas kernels: 98.5 us -> 95.1 us  [on_device(): pl.pallas_call(functools.partial(kernel, nodes, replicas, chunk), out_sha...]
where the time goes in v2:
time: 97.5 us; the launch traced here: 97.3 us
  Pallas kernels  95.1 us (98%)
  local copies, waits for them, and re-layouts  2.16 us (2%)
    pallas_call x1, Pallas kernels, on_device(): pl.pallas_call(functools.partial(kernel, nodes, replicas, chunk), out_sha...  95.1 us
    unnamed x2, local copies, waits for them, and re-layouts  2.16 us

profile of v2, /device:TPU:0, one launch (start us, length us, event | category | flops | bytes accessed | tf_op | source)
XLA Modules:
  0.0 97.3 jit_solution(11843632023553282400)
XLA Ops:
  0.0 1.1 %copy.4.scales = f32[1024,20]{1,0:T(8,128)S(1)} copy(f32[1024,20]{0,1:T(8,128)} %param.5) | data formatting | bytes 163840 | tf_op args[2]
  1.1 95.1 %shard_map.37 = f32[128,2560]{1,0:T(8,128)S(1)} custom-call(bf16[256,4096]{1,0:T(8,128)(2,1)} %hidden.1, bf16[256,2560]{1,0:T(8,128)(2,1)} %cotangent.1, f32[1024,20]{1,0:T(8,128)S(1)} %copy.4.scales), custom_call_target="tpu_custom_call" | custom-call | flops 5368709120 | bytes 3407872 | tf_op jit(solution)/shard_map/pallas_call | solution.py:334
  96.3 1.1 %copy.6 = f32[128,2560]{1,0:T(8,128)} copy(f32[128,2560]{1,0:T(8,128)S(1)} %shard_map.37) | data formatting | bytes 2621440

commit v3 on v2

--- a/solution.py
+++ b/solution.py
@@ -19,7 +19,7 @@
 def kernel(
     nodes, replicas, chunk,
     hidden, cotangent, scales, out,
-    hid, hid_t, cot, table, inverse, forward, levels, partner_in, pair, arrived, relay_in, merged,
+    raw, hid, hid_t, cot, table, stage, inverse, forward, spread_inverse, levels, partner_in, pair, arrived, relay_in, merged,
     local_sem, hid_send, hid_recv, cot_send, cot_recv, pair_send, pair_recv, z_send, z_recv,
     forward_send, forward_recv, relay_send, relay_recv, cross_send, cross_recv,
 ):
@@ -30,7 +30,7 @@
     rows = slab // nodes
     final = rows // replicas
     tile = 2 * final
-    scale_cols = scales.shape[1]
+    scale_cols = scales.shape[0]
     node = lax.axis_index("node")
     replica = lax.axis_index("replica")
     chip = replica // 2
@@ -69,9 +69,11 @@
         begin = pl.multiple_of(node * rows, BLOCK)
         return pltpu.make_async_copy(hidden.at[:, pl.ds(begin, rows)], hid.at[0], local_sem.at[0])
 
-    def own_cot(j):
-        begin = pl.multiple_of(j * chunk, BLOCK)
-        return pltpu.make_async_copy(cotangent.at[:, pl.ds(begin, chunk)], cot.at[j, 0], local_sem.at[1 + j])
+    def own_cot():
+        return pltpu.make_async_copy(cotangent, raw, local_sem.at[1])
+
+    def slot(step):
+        return slice(step * tokens, (step + 1) * tokens)
 
     def hid_copy(step):
         to = peer_node(step)
@@ -82,17 +84,17 @@
         )
 
     def cot_copy(j, step):
-        begin = pl.multiple_of(j * chunk, BLOCK)
-        return pltpu.make_async_remote_copy(
-            cotangent.at[:, pl.ds(begin, chunk)], cot.at[j, step],
+        return pltpu.make_async_remote_copy(
+            cot.at[j, slot(0)], cot.at[j, slot(step)],
             cot_send.at[j, step - 1], cot_recv.at[j, step - 1],
             device_id={"node": peer_node(step)}, device_id_type=MESH,
         )
 
     def forward_copy(j, way):
-        span = slice(way * (tokens // 2), (way + 1) * (tokens // 2))
-        return pltpu.make_async_remote_copy(
-            cot.at[j, 1 + way, span], cot.at[j, 3, span], forward_send.at[j, way], forward_recv.at[j, way],
+        part = tokens // 2
+        return pltpu.make_async_remote_copy(
+            cot.at[j, pl.ds((1 + way) * tokens + way * part, part)],
+            cot.at[j, pl.ds(3 * tokens + way * part, part)], forward_send.at[j, way], forward_recv.at[j, way],
             device_id={"node": peer_node(2 - way)}, device_id_type=MESH,
         )
 
@@ -145,9 +147,7 @@
 
     own_hidden().start()
 
-    @pl.loop(0, chunks)
-    def _(j):
-        own_cot(j).start()
+    own_cot().start()
 
     pl.semaphore_wait(barrier, nodes - 1 + chips)
     for step in range(1, nodes):
@@ -156,9 +156,6 @@
     def send_cot(j):
         for step in direct:
             cot_copy(j, step).start()
-
-    for j in range(AHEAD):
-        send_cot(j)
 
     row_index = lax.broadcasted_iota(jnp.int32, (chunk, chunk), 0)
     col_index = lax.broadcasted_iota(jnp.int32, (chunk, chunk), 1)
@@ -169,17 +166,6 @@
     same = jnp.right_shift(row_index, 7) == jnp.right_shift(col_index, 7)
     table[...] = jnp.where(same, signs, 0.0).astype(jnp.bfloat16)
 
-    def split_store(ref, value):
-        high = value.astype(jnp.bfloat16)
-        low = (value - high.astype(jnp.float32)).astype(jnp.bfloat16)
-        ref[...] = jnp.zeros_like(ref)
-        ref[:, :scale_cols] = high
-        ref[:, BLOCK:BLOCK + scale_cols] = low
-
-    norm = 1.0 / math.sqrt(BLOCK)
-    split_store(inverse, norm / scales[...])
-    split_store(forward, norm * scales[...])
-
     def spread(j):
         source = lax.broadcasted_iota(jnp.int32, (2 * BLOCK, chunk), 0)
         target = lax.broadcasted_iota(jnp.int32, (2 * BLOCK, chunk), 1)
@@ -193,6 +179,34 @@
         high = value.astype(jnp.bfloat16)
         low = (value - high.astype(jnp.float32)).astype(jnp.bfloat16)
         return mul(high, table[...]) + mul(low, table[...])
+
+    own_cot().wait()
+
+    @pl.loop(0, chunks)
+    def _(j):
+        block = raw[:, pl.ds(pl.multiple_of(j * chunk, BLOCK), chunk)]
+        cot[j, slot(0)] = mul(block, table[...]).astype(jnp.bfloat16)
+
+    for j in range(AHEAD):
+        send_cot(j)
+
+    def split_store(ref, value):
+        stage[...] = jnp.zeros_like(stage)
+        stage[:scale_cols, :] = value
+        for part in range(rows // BLOCK):
+            span = slice(part * BLOCK, (part + 1) * BLOCK)
+            turned = stage[:, span].T
+            high = turned.astype(jnp.bfloat16)
+            ref[span, :BLOCK] = high
+            ref[span, BLOCK:] = (turned - high.astype(jnp.float32)).astype(jnp.bfloat16)
+
+    norm = 1.0 / math.sqrt(BLOCK)
+    split_store(inverse, norm / scales[...])
+    split_store(forward, norm * scales[...])
+
+    @pl.loop(0, chunks)
+    def _(j):
+        spread_inverse[j] = mul(inverse[...], spread(j))
 
     for step in range(nodes):
         if step == 0:
@@ -204,7 +218,7 @@
                 send_cot(j)
         for part in range(rows // BLOCK):
             span = slice(part * BLOCK, (part + 1) * BLOCK)
-            hid_t[step, span, :] = hid[step, :, span].T
+            hid_t[span, slot(step)] = hid[step, :, span].T
         if square and step >= nodes - AHEAD:
             pass_on(step - (nodes - AHEAD))
 
@@ -228,7 +242,6 @@
         def _():
             send_cot(j + WINDOW)
 
-        own_cot(j).wait()
         if square:
             @pl.when(j + AHEAD < chunks)
             def _():
@@ -239,20 +252,14 @@
         else:
             for step in direct:
                 cot_copy(j, step).wait_recv()
-        expand = spread(j)
 
         for half, (first, count) in enumerate(halves):
-            @pl.loop(first, first + count)
-            def _(z):
-                span = pl.ds(pl.multiple_of(z * tile, tile), tile)
-                total = None
-                for step in range(nodes):
-                    term = mul(hid_t[step, span, :], cot[j, step]).astype(jnp.bfloat16).astype(jnp.float32)
-                    total = term if total is None else total + term
-                level = rotate(total) * mul(inverse[span, :], expand)
-                level = jnp.clip(level, -7.0, 7.0).astype(jnp.bfloat16)
-                levels[j, 0, z] = level[:final]
-                levels[j, 1, z] = level[final:]
+            span = pl.ds(pl.multiple_of(first * tile, tile), count * tile)
+            level = mul(hid_t[span, :], cot[j]) * spread_inverse[j, span]
+            level = jnp.clip(level, -7.0, 7.0).astype(jnp.bfloat16)
+            for z in range(count):
+                levels[j, 0, first + z] = level[z * tile:z * tile + final]
+                levels[j, 1, first + z] = level[z * tile + final:(z + 1) * tile]
 
             pair_copy(j, half).start()
 
@@ -341,19 +348,22 @@
         ],
         out_specs=pl.BlockSpec(memory_space=pltpu.VMEM),
         scratch_shapes=[
+            pltpu.VMEM((tokens, width), bf16),
             pltpu.VMEM((nodes, tokens, rows), bf16),
-            pltpu.VMEM((nodes, rows, tokens), bf16),
-            pltpu.VMEM((chunks, nodes, tokens, chunk), bf16),
+            pltpu.VMEM((rows, nodes * tokens), bf16),
+            pltpu.VMEM((chunks, nodes * tokens, chunk), bf16),
             pltpu.VMEM((chunk, chunk), bf16),
+            pltpu.VMEM((BLOCK, rows), jnp.float32),
             pltpu.VMEM((rows, 2 * BLOCK), bf16),
             pltpu.VMEM((rows, 2 * BLOCK), bf16),
+            pltpu.VMEM((chunks, rows, chunk), jnp.float32),
             pltpu.VMEM((chunks, 2, chips, final, chunk), bf16),
             pltpu.VMEM((chunks, chips, final, chunk), bf16),
             pltpu.VMEM((chunks, chips, final, chunk), bf16),
             pltpu.VMEM((chunks, slots, final, chunk), bf16),
             pltpu.VMEM((chunks, 2, final, chunk), bf16),
             pltpu.VMEM((chunks, 2, final, chunk), bf16),
-            dma((1 + chunks,)),
+            dma((2,)),
             dma((nodes - 1,)),
             dma((nodes - 1,)),
             dma((chunks, nodes - 1)),
@@ -375,7 +385,7 @@
         cost_estimate=pl.CostEstimate(
             flops=2 * tokens * slab * width, bytes_accessed=2 * tokens * (slab + width), transcendentals=0
         ),
-    )(hidden, cotangent, scales)
+    )(hidden, cotangent, scales.T)
 
 
 def solution(mesh):

time: 97.5 us -> 96.9 us (level)
    unnamed x2 -> x3, local copies, waits for them, and re-layouts: 2.16 us -> 1.95 us
where the time goes in v3:
time: 96.9 us; the launch traced here: 96.8 us
  Pallas kernels  94.8 us (98%)
  local copies, waits for them, and re-layouts  1.95 us (2%)
    pallas_call x1, Pallas kernels, on_device(): pl.pallas_call(functools.partial(kernel, nodes, replicas, chunk), out_sha...  94.8 us
    unnamed x3, local copies, waits for them, and re-layouts  1.95 us

profile of v3, /device:TPU:0, one launch (start us, length us, event | category | flops | bytes accessed | tf_op | source)
XLA Modules:
  0.0 96.8 jit_solution(11073668029816763344)
XLA Ops:
  0.0 0.0 copy-start
  0.0 0.9 copy-done
  0.9 94.8 %shard_map.37 = f32[128,2560]{1,0:T(8,128)S(1)} custom-call(bf16[256,4096]{1,0:T(8,128)(2,1)} %hidden.1, bf16[256,2560]{1,0:T(8,128)(2,1)} %cotangent.1, f32[20,1024]{1,0:T(8,128)S(1)} %bitcast.1), custom_call_target="tpu_custom_call" | custom-call | flops 5368709120 | bytes 3407872 | tf_op jit(solution)/shard_map/pallas_call | solution.py:341
  95.7 1.1 %copy.5 = f32[128,2560]{1,0:T(8,128)} copy(f32[128,2560]{1,0:T(8,128)S(1)} %shard_map.37) | data formatting | bytes 2621440
Async XLA Ops:
  0.0 0.9 copy-start

commit v4 on v3

--- a/solution.py
+++ b/solution.py
@@ -10,16 +10,17 @@
 
 MESH = pl.DeviceIdType.MESH
 BLOCK = 128
-WINDOW = 4
-AHEAD = 2
-RELAY_LAG = 2
-FINISH_LAG = 4
+WINDOW = 8
+AHEAD = 4
+PAIR_LAG = 1
+RELAY_LAG = 4
+FINISH_LAG = 8
 
 
 def kernel(
     nodes, replicas, chunk,
     hidden, cotangent, scales, out,
-    raw, hid, hid_t, cot, table, stage, inverse, forward, spread_inverse, levels, partner_in, pair, arrived, relay_in, merged,
+    raw, scale, hid, hid_t, cot, table, stage, inverse, forward, spread_inverse, levels, partner_in, pair, arrived, relay_in, merged,
     local_sem, hid_send, hid_recv, cot_send, cot_recv, pair_send, pair_recv, z_send, z_recv,
     forward_send, forward_recv, relay_send, relay_recv, cross_send, cross_recv,
 ):
@@ -148,6 +149,8 @@
     own_hidden().start()
 
     own_cot().start()
+    own_scales = pltpu.make_async_copy(scales, scale, local_sem.at[2])
+    own_scales.start()
 
     pl.semaphore_wait(barrier, nodes - 1 + chips)
     for step in range(1, nodes):
@@ -201,8 +204,9 @@
             ref[span, BLOCK:] = (turned - high.astype(jnp.float32)).astype(jnp.bfloat16)
 
     norm = 1.0 / math.sqrt(BLOCK)
-    split_store(inverse, norm / scales[...])
-    split_store(forward, norm * scales[...])
+    own_scales.wait()
+    split_store(inverse, norm / scale[...])
+    split_store(forward, norm * scale[...])
 
     @pl.loop(0, chunks)
     def _(j):
@@ -219,8 +223,9 @@
         for part in range(rows // BLOCK):
             span = slice(part * BLOCK, (part + 1) * BLOCK)
             hid_t[span, slot(step)] = hid[step, :, span].T
-        if square and step >= nodes - AHEAD:
-            pass_on(step - (nodes - AHEAD))
+        if square and step >= 2:
+            for k in range(AHEAD // 2):
+                pass_on((step - 2) * (AHEAD // 2) + k)
 
     own_rows = pl.ds(pl.multiple_of(replica * final, final), final)
 
@@ -236,6 +241,26 @@
         total = total * mul(forward[own_rows, :], spread(j))
         out[:, pl.ds(pl.multiple_of(j * chunk, BLOCK), chunk)] = rotate(total)
 
+    def combine(j):
+        for half, (first, count) in enumerate(halves):
+            pair_copy(j, half).wait_recv()
+
+            @pl.loop(first, first + count)
+            def _(z):
+                both = levels[j, core, z].astype(jnp.float32) + partner_in[j, z].astype(jnp.float32)
+                pair[j, z] = both.astype(jnp.bfloat16)
+
+            if line and half == 0:
+                @pl.when(edge)
+                def _():
+                    relay_copy(j).start()
+
+        if line:
+            mate_copy(j).start()
+        else:
+            for step in range(1, chips):
+                z_copy(j, step).start()
+
     @pl.loop(0, chunks)
     def _(j):
         @pl.when(j + WINDOW < chunks)
@@ -263,32 +288,21 @@
 
             pair_copy(j, half).start()
 
-        for half, (first, count) in enumerate(halves):
-            pair_copy(j, half).wait_recv()
-
-            @pl.loop(first, first + count)
-            def _(z):
-                both = levels[j, core, z].astype(jnp.float32) + partner_in[j, z].astype(jnp.float32)
-                pair[j, z] = both.astype(jnp.bfloat16)
-
-            if line and half == 0:
-                @pl.when(edge)
-                def _():
-                    relay_copy(j).start()
+        @pl.when(j >= PAIR_LAG)
+        def _():
+            combine(j - PAIR_LAG)
 
         if line:
-            mate_copy(j).start()
-
             @pl.when(j >= RELAY_LAG)
             def _():
                 relay(j - RELAY_LAG)
-        else:
-            for step in range(1, chips):
-                z_copy(j, step).start()
 
         @pl.when(j >= FINISH_LAG)
         def _():
             finish(j - FINISH_LAG)
+
+    for j in range(chunks - PAIR_LAG, chunks):
+        combine(j)
 
     if line:
         @pl.loop(chunks - RELAY_LAG, chunks)
@@ -330,7 +344,7 @@
 def on_device(nodes, replicas, hidden, cotangent, scales):
     tokens, slab = hidden.shape
     width = cotangent.shape[1]
-    chunk = 2 * BLOCK
+    chunk = BLOCK
     chunks = width // chunk
     rows = slab // nodes
     final = rows // replicas
@@ -344,11 +358,12 @@
         in_specs=[
             pl.BlockSpec(memory_space=pl.ANY),
             pl.BlockSpec(memory_space=pl.ANY),
-            pl.BlockSpec(memory_space=pltpu.VMEM),
+            pl.BlockSpec(memory_space=pl.ANY),
         ],
         out_specs=pl.BlockSpec(memory_space=pltpu.VMEM),
         scratch_shapes=[
             pltpu.VMEM((tokens, width), bf16),
+            pltpu.VMEM((scales.shape[1], rows), jnp.float32),
             pltpu.VMEM((nodes, tokens, rows), bf16),
             pltpu.VMEM((rows, nodes * tokens), bf16),
             pltpu.VMEM((chunks, nodes * tokens, chunk), bf16),
@@ -363,7 +378,7 @@
             pltpu.VMEM((chunks, slots, final, chunk), bf16),
             pltpu.VMEM((chunks, 2, final, chunk), bf16),
             pltpu.VMEM((chunks, 2, final, chunk), bf16),
-            dma((2,)),
+            dma((3,)),
             dma((nodes - 1,)),
             dma((nodes - 1,)),
             dma((chunks, nodes - 1)),

time: 96.9 us -> 98.9 us (1.021)
  Pallas kernels: 94.8 us -> 96.8 us
    pallas_call x1, Pallas kernels: 94.8 us -> 96.8 us  [on_device(): pl.pallas_call(functools.partial(kernel, nodes, replicas, chunk), out_sha...]
where the time goes in v4:
time: 98.9 us; the launch traced here: 98.7 us
  Pallas kernels  96.8 us (98%)
  local copies, waits for them, and re-layouts  1.95 us (2%)
    pallas_call x1, Pallas kernels, on_device(): pl.pallas_call(functools.partial(kernel, nodes, replicas, chunk), out_sha...  96.8 us

profile of v4, /device:TPU:0, one launch (start us, length us, event | category | flops | bytes accessed | tf_op | source)
XLA Modules:
  0.0 98.7 jit_solution(6987209560898520834)
XLA Ops:
  0.0 0.0 copy-start
  0.0 0.9 copy-done
  0.9 96.8 %shard_map.37 = f32[128,2560]{1,0:T(8,128)S(1)} custom-call(bf16[256,4096]{1,0:T(8,128)(2,1)} %hidden.1, bf16[256,2560]{1,0:T(8,128)(2,1)} %cotangent.1, f32[20,1024]{1,0:T(8,128)S(1)} %bitcast.1), custom_call_target="tpu_custom_call" | custom-call | flops 5368709120 | bytes 3407872 | tf_op jit(solution)/shard_map/pallas_call | solution.py:355
  97.7 1.1 %copy.5 = f32[128,2560]{1,0:T(8,128)} copy(f32[128,2560]{1,0:T(8,128)S(1)} %shard_map.37) | data formatting | bytes 2621440
Async XLA Ops:
  0.0 0.9 copy-start

commit v5 on v4

--- a/solution.py
+++ b/solution.py
@@ -10,11 +10,11 @@
 
 MESH = pl.DeviceIdType.MESH
 BLOCK = 128
-WINDOW = 8
-AHEAD = 4
-PAIR_LAG = 1
-RELAY_LAG = 4
-FINISH_LAG = 8
+WINDOW = 4
+AHEAD = 2
+PAIR_LAG = 0
+RELAY_LAG = 2
+FINISH_LAG = 4
 
 
 def kernel(
@@ -153,7 +153,7 @@
     own_scales.start()
 
     pl.semaphore_wait(barrier, nodes - 1 + chips)
-    for step in range(1, nodes):
+    for step in reversed(range(1, nodes)):
         hid_copy(step).start()
 
     def send_cot(j):
@@ -189,9 +189,6 @@
     def _(j):
         block = raw[:, pl.ds(pl.multiple_of(j * chunk, BLOCK), chunk)]
         cot[j, slot(0)] = mul(block, table[...]).astype(jnp.bfloat16)
-
-    for j in range(AHEAD):
-        send_cot(j)
 
     def split_store(ref, value):
         stage[...] = jnp.zeros_like(stage)
@@ -212,20 +209,28 @@
     def _(j):
         spread_inverse[j] = mul(inverse[...], spread(j))
 
-    for step in range(nodes):
-        if step == 0:
-            own_hidden().wait()
-        else:
-            hid_copy(step).wait_recv()
-        if step == 1:
-            for j in range(AHEAD, WINDOW):
-                send_cot(j)
+    def turn(step):
         for part in range(rows // BLOCK):
             span = slice(part * BLOCK, (part + 1) * BLOCK)
             hid_t[span, slot(step)] = hid[step, :, span].T
-        if square and step >= 2:
-            for k in range(AHEAD // 2):
-                pass_on((step - 2) * (AHEAD // 2) + k)
+
+    own_hidden().wait()
+    turn(0)
+    for step in direct:
+        hid_copy(step).wait_recv()
+    for j in range(AHEAD):
+        send_cot(j)
+    for step in direct:
+        turn(step)
+    if square:
+        hid_copy(3).wait_recv()
+        for j in range(AHEAD):
+            pass_on(j)
+            send_cot(j + AHEAD)
+        turn(3)
+    else:
+        for j in range(AHEAD, WINDOW):
+            send_cot(j)
 
     own_rows = pl.ds(pl.multiple_of(replica * final, final), final)
 
@@ -263,15 +268,16 @@
 
     @pl.loop(0, chunks)
     def _(j):
-        @pl.when(j + WINDOW < chunks)
-        def _():
-            send_cot(j + WINDOW)
-
         if square:
             @pl.when(j + AHEAD < chunks)
             def _():
                 pass_on(j + AHEAD)
 
+        @pl.when(j + WINDOW < chunks)
+        def _():
+            send_cot(j + WINDOW)
+
+        if square:
             for way in range(2):
                 forward_copy(j, way).wait_recv()
         else:
@@ -344,7 +350,7 @@
 def on_device(nodes, replicas, hidden, cotangent, scales):
     tokens, slab = hidden.shape
     width = cotangent.shape[1]
-    chunk = BLOCK
+    chunk = 2 * BLOCK
     chunks = width // chunk
     rows = slab // nodes
     final = rows // replicas

time: 98.9 us -> 96.1 us (0.972)
  Pallas kernels: 96.8 us -> 94 us
    pallas_call x1, Pallas kernels: 96.8 us -> 94 us  [on_device(): pl.pallas_call(functools.partial(kernel, nodes, replicas, chunk), out_sha...]
where the time goes in v5:
time: 96.1 us; the launch traced here: 95.9 us
  Pallas kernels  94 us (98%)
  local copies, waits for them, and re-layouts  1.95 us (2%)
    pallas_call x1, Pallas kernels, on_device(): pl.pallas_call(functools.partial(kernel, nodes, replicas, chunk), out_sha...  94 us
    unnamed x3, local copies, waits for them, and re-layouts  1.95 us

profile of v5, /device:TPU:0, one launch (start us, length us, event | category | flops | bytes accessed | tf_op | source)
XLA Modules:
  0.0 95.9 jit_solution(13492057873155036410)
XLA Ops:
  0.0 0.0 copy-start
  0.0 0.9 copy-done
  0.9 94.0 %shard_map.37 = f32[128,2560]{1,0:T(8,128)S(1)} custom-call(bf16[256,4096]{1,0:T(8,128)(2,1)} %hidden.1, bf16[256,2560]{1,0:T(8,128)(2,1)} %cotangent.1, f32[20,1024]{1,0:T(8,128)S(1)} %bitcast.1), custom_call_target="tpu_custom_call" | custom-call | flops 5368709120 | bytes 3407872 | tf_op jit(solution)/shard_map/pallas_call | solution.py:361
  94.9 1.1 %copy.5 = f32[128,2560]{1,0:T(8,128)} copy(f32[128,2560]{1,0:T(8,128)S(1)} %shard_map.37) | data formatting | bytes 2621440
Async XLA Ops:
  0.0 0.9 copy-start

commit v6 on v5

--- a/solution.py
+++ b/solution.py
@@ -12,7 +12,7 @@
 BLOCK = 128
 WINDOW = 4
 AHEAD = 2
-PAIR_LAG = 0
+LATE_HIDDEN = 3
 RELAY_LAG = 2
 FINISH_LAG = 4
 
@@ -47,7 +47,8 @@
     inner = lax.rem(chip, 2) == 1 - side
     edge = lax.rem(chip, 2) == side
     direct = (1, 2) if square else tuple(range(1, nodes))
-    halves = ((far, 2), (2 * side, 2)) if line else ((0, chips),)
+    parts = ((far, 2), (mate, 1), (chip, 1)) if line else ((0, chips),)
+    early = parts[:2]
 
     def peer_node(step):
         if square:
@@ -76,13 +77,20 @@
     def slot(step):
         return slice(step * tokens, (step + 1) * tokens)
 
-    def hid_copy(step):
+    def hid_copy(step, part):
         to = peer_node(step)
-        begin = pl.multiple_of(to * rows, BLOCK)
-        return pltpu.make_async_remote_copy(
-            hidden.at[:, pl.ds(begin, rows)], hid.at[step], hid_send.at[step - 1], hid_recv.at[step - 1],
+        first, count = parts[part]
+        source = pl.multiple_of(to * rows + first * tile, BLOCK)
+        target = pl.multiple_of(first * tile, BLOCK)
+        return pltpu.make_async_remote_copy(
+            hidden.at[:, pl.ds(source, count * tile)], hid.at[step, :, pl.ds(target, count * tile)],
+            hid_send.at[step - 1, part], hid_recv.at[step - 1, part],
             device_id={"node": to}, device_id_type=MESH,
         )
+
+    def send_hid(part):
+        for step in reversed(range(1, nodes)):
+            hid_copy(step, part).start()
 
     def cot_copy(j, step):
         return pltpu.make_async_remote_copy(
@@ -105,7 +113,7 @@
             forward_copy(j, way).start()
 
     def pair_copy(j, half):
-        first, count = halves[half]
+        first, count = parts[half]
         return pltpu.make_async_remote_copy(
             levels.at[j, 1 - core, pl.ds(first, count)], partner_in.at[j, pl.ds(first, count)],
             pair_send.at[j, half], pair_recv.at[j, half],
@@ -153,8 +161,8 @@
     own_scales.start()
 
     pl.semaphore_wait(barrier, nodes - 1 + chips)
-    for step in reversed(range(1, nodes)):
-        hid_copy(step).start()
+    for part in range(len(early)):
+        send_hid(part)
 
     def send_cot(j):
         for step in direct:
@@ -209,25 +217,31 @@
     def _(j):
         spread_inverse[j] = mul(inverse[...], spread(j))
 
-    def turn(step):
-        for part in range(rows // BLOCK):
-            span = slice(part * BLOCK, (part + 1) * BLOCK)
+    def turn(step, part):
+        first, count = parts[part]
+        for piece in range(count * tile // BLOCK):
+            span = pl.ds(pl.multiple_of(first * tile + piece * BLOCK, BLOCK), BLOCK)
             hid_t[span, slot(step)] = hid[step, :, span].T
 
     own_hidden().wait()
-    turn(0)
-    for step in direct:
-        hid_copy(step).wait_recv()
+    for part in range(len(parts)):
+        turn(0, part)
+    for part in range(len(early)):
+        for step in direct:
+            hid_copy(step, part).wait_recv()
     for j in range(AHEAD):
         send_cot(j)
-    for step in direct:
-        turn(step)
+    for part in range(len(early)):
+        for step in direct:
+            turn(step, part)
     if square:
-        hid_copy(3).wait_recv()
+        for part in range(len(early)):
+            hid_copy(3, part).wait_recv()
         for j in range(AHEAD):
             pass_on(j)
             send_cot(j + AHEAD)
-        turn(3)
+        for part in range(len(early)):
+            turn(3, part)
     else:
         for j in range(AHEAD, WINDOW):
             send_cot(j)
@@ -235,27 +249,38 @@
     own_rows = pl.ds(pl.multiple_of(replica * final, final), final)
 
     def finish(j):
-        total = pair[j, chip].astype(jnp.float32)
         if line:
+            pair_copy(j, 2).wait_recv()
             mate_copy(j).wait_recv()
             cross_copy(j, 0).wait_recv()
-        for slot in range(arrived.shape[1]):
+            total = levels[j, core, chip].astype(jnp.float32) + partner_in[j, chip].astype(jnp.float32)
+        else:
+            total = pair[j, chip].astype(jnp.float32)
+        for k in range(arrived.shape[1]):
             if not line:
-                z_copy(j, slot + 1).wait_recv()
-            total = total + arrived[j, slot].astype(jnp.float32)
+                z_copy(j, k + 1).wait_recv()
+            total = total + arrived[j, k].astype(jnp.float32)
         total = total * mul(forward[own_rows, :], spread(j))
         out[:, pl.ds(pl.multiple_of(j * chunk, BLOCK), chunk)] = rotate(total)
 
+    def product(j, part):
+        first, count = parts[part]
+        span = pl.ds(pl.multiple_of(first * tile, tile), count * tile)
+        level = mul(hid_t[span, :], cot[j]) * spread_inverse[j, span]
+        level = jnp.clip(level, -7.0, 7.0).astype(jnp.bfloat16)
+        for z in range(count):
+            levels[j, 0, first + z] = level[z * tile:z * tile + final]
+            levels[j, 1, first + z] = level[z * tile + final:(z + 1) * tile]
+        pair_copy(j, part).start()
+
     def combine(j):
-        for half, (first, count) in enumerate(halves):
-            pair_copy(j, half).wait_recv()
-
-            @pl.loop(first, first + count)
-            def _(z):
-                both = levels[j, core, z].astype(jnp.float32) + partner_in[j, z].astype(jnp.float32)
-                pair[j, z] = both.astype(jnp.bfloat16)
-
-            if line and half == 0:
+        for part, (first, count) in enumerate(early):
+            pair_copy(j, part).wait_recv()
+            for z in range(count):
+                both = levels[j, core, first + z].astype(jnp.float32) + partner_in[j, first + z].astype(jnp.float32)
+                pair[j, first + z] = both.astype(jnp.bfloat16)
+
+            if line and part == 0:
                 @pl.when(edge)
                 def _():
                     relay_copy(j).start()
@@ -284,43 +309,48 @@
             for step in direct:
                 cot_copy(j, step).wait_recv()
 
-        for half, (first, count) in enumerate(halves):
-            span = pl.ds(pl.multiple_of(first * tile, tile), count * tile)
-            level = mul(hid_t[span, :], cot[j]) * spread_inverse[j, span]
-            level = jnp.clip(level, -7.0, 7.0).astype(jnp.bfloat16)
-            for z in range(count):
-                levels[j, 0, first + z] = level[z * tile:z * tile + final]
-                levels[j, 1, first + z] = level[z * tile + final:(z + 1) * tile]
-
-            pair_copy(j, half).start()
-
-        @pl.when(j >= PAIR_LAG)
-        def _():
-            combine(j - PAIR_LAG)
+        if line:
+            @pl.when(j == chunks - LATE_HIDDEN)
+            def _():
+                send_hid(2)
+
+        for part in range(len(early)):
+            product(j, part)
+        combine(j)
 
         if line:
             @pl.when(j >= RELAY_LAG)
             def _():
                 relay(j - RELAY_LAG)
-
-        @pl.when(j >= FINISH_LAG)
-        def _():
-            finish(j - FINISH_LAG)
-
-    for j in range(chunks - PAIR_LAG, chunks):
-        combine(j)
+        else:
+            @pl.when(j >= FINISH_LAG)
+            def _():
+                finish(j - FINISH_LAG)
 
     if line:
         @pl.loop(chunks - RELAY_LAG, chunks)
         def _(j):
             relay(j)
 
+        for step in range(1, nodes):
+            hid_copy(step, 2).wait_recv()
+            turn(step, 2)
+
+        @pl.loop(0, chunks)
+        def _(j):
+            product(j, 2)
+
+            @pl.when(j >= FINISH_LAG)
+            def _():
+                finish(j - FINISH_LAG)
+
     @pl.loop(chunks - FINISH_LAG, chunks)
     def _(j):
         finish(j)
 
     for step in range(1, nodes):
-        hid_copy(step).wait_send()
+        for part in range(len(parts)):
+            hid_copy(step, part).wait_send()
 
     @pl.loop(0, chunks)
     def _(j):
@@ -329,7 +359,7 @@
         if square:
             for way in range(2):
                 forward_copy(j, way).wait_send()
-        for half in range(len(halves)):
+        for half in range(len(parts)):
             pair_copy(j, half).wait_send()
         if line:
             mate_copy(j).wait_send()
@@ -385,12 +415,12 @@
             pltpu.VMEM((chunks, 2, final, chunk), bf16),
             pltpu.VMEM((chunks, 2, final, chunk), bf16),
             dma((3,)),
-            dma((nodes - 1,)),
-            dma((nodes - 1,)),
+            dma((nodes - 1, 3)),
+            dma((nodes - 1, 3)),
             dma((chunks, nodes - 1)),
             dma((chunks, nodes - 1)),
-            dma((chunks, 2)),
-            dma((chunks, 2)),
+            dma((chunks, 3)),
+            dma((chunks, 3)),
             dma((chunks, slots)),
             dma((chunks, slots)),
             dma((chunks, 2)),

time: 96.1 us -> 91.1 us (0.948)
  Pallas kernels: 94 us -> 88.1 us
    pallas_call x1, Pallas kernels: 94 us -> 88.1 us  [on_device(): pl.pallas_call(functools.partial(kernel, nodes, replicas, chunk), out_sha...]
where the time goes in v6:
time: 91.1 us; the launch traced here: 90 us
  Pallas kernels  88.1 us (97%)
  local copies, waits for them, and re-layouts  1.95 us (2%)
    pallas_call x1, Pallas kernels, on_device(): pl.pallas_call(functools.partial(kernel, nodes, replicas, chunk), out_sha...  88.1 us
    unnamed x3, local copies, waits for them, and re-layouts  1.95 us

profile of v6, /device:TPU:0, one launch (start us, length us, event | category | flops | bytes accessed | tf_op | source)
XLA Modules:
  0.0 90.0 jit_solution(3026097101753042746)
XLA Ops:
  0.0 0.0 copy-start
  0.0 0.9 copy-done
  0.9 88.1 %shard_map.37 = f32[128,2560]{1,0:T(8,128)S(1)} custom-call(bf16[256,4096]{1,0:T(8,128)(2,1)} %hidden.1, bf16[256,2560]{1,0:T(8,128)(2,1)} %cotangent.1, f32[20,1024]{1,0:T(8,128)S(1)} %bitcast.1), custom_call_target="tpu_custom_call" | custom-call | flops 5368709120 | bytes 3407872 | tf_op jit(solution)/shard_map/pallas_call | solution.py:391
  89.0 1.1 %copy.5 = f32[128,2560]{1,0:T(8,128)} copy(f32[128,2560]{1,0:T(8,128)S(1)} %shard_map.37) | data formatting | bytes 2621440
Async XLA Ops:
  0.0 0.9 copy-start

commit v7 on v6

--- a/solution.py
+++ b/solution.py
@@ -10,11 +10,12 @@
 
 MESH = pl.DeviceIdType.MESH
 BLOCK = 128
-WINDOW = 4
-AHEAD = 2
-LATE_HIDDEN = 3
-RELAY_LAG = 2
-FINISH_LAG = 4
+WINDOW = 8
+AHEAD = 4
+LATE_HIDDEN = 6
+PAIR_LAG = 1
+RELAY_LAG = 4
+FINISH_LAG = 8
 
 
 def kernel(
@@ -316,7 +317,10 @@
 
         for part in range(len(early)):
             product(j, part)
-        combine(j)
+
+        @pl.when(j >= PAIR_LAG)
+        def _():
+            combine(j - PAIR_LAG)
 
         if line:
             @pl.when(j >= RELAY_LAG)
@@ -326,6 +330,9 @@
             @pl.when(j >= FINISH_LAG)
             def _():
                 finish(j - FINISH_LAG)
+
+    for j in range(chunks - PAIR_LAG, chunks):
+        combine(j)
 
     if line:
         @pl.loop(chunks - RELAY_LAG, chunks)
@@ -380,7 +387,7 @@
 def on_device(nodes, replicas, hidden, cotangent, scales):
     tokens, slab = hidden.shape
     width = cotangent.shape[1]
-    chunk = 2 * BLOCK
+    chunk = BLOCK
     chunks = width // chunk
     rows = slab // nodes
     final = rows // replicas

time: 91.1 us -> 98.7 us (1.083)
  the two profiles are of different devices: /device:TPU:0 before, /device:TPU:8 now
where the time goes in v7:
time: 98.7 us; the launch traced here: 98.6 us
  Pallas kernels  96.6 us (98%)
  local copies, waits for them, and re-layouts  1.95 us (2%)
    pallas_call x1, Pallas kernels, on_device(): pl.pallas_call(functools.partial(kernel, nodes, replicas, chunk), out_sha...  96.6 us

profile of v7, /device:TPU:8, one launch (start us, length us, event | category | flops | bytes accessed | tf_op | source)
XLA Modules:
  0.0 98.6 jit_solution(12327773050149733897)
XLA Ops:
  0.0 0.0 copy-start
  0.0 0.9 copy-done
  0.9 96.6 %shard_map.37 = f32[128,2560]{1,0:T(8,128)S(1)} custom-call(bf16[256,4096]{1,0:T(8,128)(2,1)} %hidden.1, bf16[256,2560]{1,0:T(8,128)(2,1)} %cotangent.1, f32[20,1024]{1,0:T(8,128)S(1)} %bitcast.1), custom_call_target="tpu_custom_call" | custom-call | flops 5368709120 | bytes 3407872 | tf_op jit(solution)/shard_map/pallas_call | solution.py:398
  97.5 1.1 %copy.5 = f32[128,2560]{1,0:T(8,128)} copy(f32[128,2560]{1,0:T(8,128)S(1)} %shard_map.37) | data formatting | bytes 2621440
Async XLA Ops:
  0.0 0.9 copy-start

commit v8 on v6

--- a/solution.py
+++ b/solution.py
@@ -14,13 +14,13 @@
 AHEAD = 2
 LATE_HIDDEN = 3
 RELAY_LAG = 2
-FINISH_LAG = 4
+LAST = 2
 
 
 def kernel(
     nodes, replicas, chunk,
     hidden, cotangent, scales, out,
-    raw, scale, hid, hid_t, cot, table, stage, inverse, forward, spread_inverse, levels, partner_in, pair, arrived, relay_in, merged,
+    raw, scale, hid, hid_t, cot, table, stage, inverse, forward, spread_inverse, spread_forward, levels, partner_in, pair, arrived, relay_in, merged,
     local_sem, hid_send, hid_recv, cot_send, cot_recv, pair_send, pair_recv, z_send, z_recv,
     forward_send, forward_recv, relay_send, relay_recv, cross_send, cross_recv,
 ):
@@ -177,6 +177,8 @@
     same = jnp.right_shift(row_index, 7) == jnp.right_shift(col_index, 7)
     table[...] = jnp.where(same, signs, 0.0).astype(jnp.bfloat16)
 
+    own_rows = pl.ds(pl.multiple_of(replica * final, final), final)
+
     def spread(j):
         source = lax.broadcasted_iota(jnp.int32, (2 * BLOCK, chunk), 0)
         target = lax.broadcasted_iota(jnp.int32, (2 * BLOCK, chunk), 1)
@@ -197,6 +199,8 @@
     def _(j):
         block = raw[:, pl.ds(pl.multiple_of(j * chunk, BLOCK), chunk)]
         cot[j, slot(0)] = mul(block, table[...]).astype(jnp.bfloat16)
+
+    send_cot(0)
 
     def split_store(ref, value):
         stage[...] = jnp.zeros_like(stage)
@@ -215,7 +219,9 @@
 
     @pl.loop(0, chunks)
     def _(j):
-        spread_inverse[j] = mul(inverse[...], spread(j))
+        expand = spread(j)
+        spread_inverse[j] = mul(inverse[...], expand)
+        spread_forward[j] = mul(forward[own_rows, :], expand)
 
     def turn(step, part):
         first, count = parts[part]
@@ -229,7 +235,9 @@
     for part in range(len(early)):
         for step in direct:
             hid_copy(step, part).wait_recv()
-    for j in range(AHEAD):
+    if square:
+        pass_on(0)
+    for j in range(1, AHEAD):
         send_cot(j)
     for part in range(len(early)):
         for step in direct:
@@ -238,29 +246,32 @@
         for part in range(len(early)):
             hid_copy(3, part).wait_recv()
         for j in range(AHEAD):
-            pass_on(j)
             send_cot(j + AHEAD)
+            if j + 1 < AHEAD:
+                pass_on(j + 1)
         for part in range(len(early)):
             turn(3, part)
     else:
         for j in range(AHEAD, WINDOW):
             send_cot(j)
 
-    own_rows = pl.ds(pl.multiple_of(replica * final, final), final)
-
-    def finish(j):
+    def await_last(j):
         if line:
             pair_copy(j, 2).wait_recv()
             mate_copy(j).wait_recv()
             cross_copy(j, 0).wait_recv()
+        else:
+            for step in range(1, chips):
+                z_copy(j, step).wait_recv()
+
+    def finish(j):
+        if line:
             total = levels[j, core, chip].astype(jnp.float32) + partner_in[j, chip].astype(jnp.float32)
         else:
             total = pair[j, chip].astype(jnp.float32)
         for k in range(arrived.shape[1]):
-            if not line:
-                z_copy(j, k + 1).wait_recv()
             total = total + arrived[j, k].astype(jnp.float32)
-        total = total * mul(forward[own_rows, :], spread(j))
+        total = total * spread_forward[j]
         out[:, pl.ds(pl.multiple_of(j * chunk, BLOCK), chunk)] = rotate(total)
 
     def product(j, part):
@@ -322,10 +333,6 @@
             @pl.when(j >= RELAY_LAG)
             def _():
                 relay(j - RELAY_LAG)
-        else:
-            @pl.when(j >= FINISH_LAG)
-            def _():
-                finish(j - FINISH_LAG)
 
     if line:
         @pl.loop(chunks - RELAY_LAG, chunks)
@@ -336,17 +343,14 @@
             hid_copy(step, 2).wait_recv()
             turn(step, 2)
 
-        @pl.loop(0, chunks)
-        def _(j):
+        for j in range(chunks):
             product(j, 2)
 
-            @pl.when(j >= FINISH_LAG)
-            def _():
-                finish(j - FINISH_LAG)
-
-    @pl.loop(chunks - FINISH_LAG, chunks)
-    def _(j):
-        finish(j)
+    for group in (range(chunks - LAST), range(chunks - LAST, chunks)):
+        for j in group:
+            await_last(j)
+        for j in group:
+            finish(j)
 
     for step in range(1, nodes):
         for part in range(len(parts)):
@@ -408,6 +412,7 @@
             pltpu.VMEM((rows, 2 * BLOCK), bf16),
             pltpu.VMEM((rows, 2 * BLOCK), bf16),
             pltpu.VMEM((chunks, rows, chunk), jnp.float32),
+            pltpu.VMEM((chunks, final, chunk), jnp.float32),
             pltpu.VMEM((chunks, 2, chips, final, chunk), bf16),
             pltpu.VMEM((chunks, chips, final, chunk), bf16),
             pltpu.VMEM((chunks, chips, final, chunk), bf16),

time: 91.1 us -> 90.1 us (0.989)
  no operation moved by 1% of the time
where the time goes in v8:
time: 90.1 us; the launch traced here: 89.9 us
  Pallas kernels  88 us (98%)
  local copies, waits for them, and re-layouts  1.95 us (2%)
    pallas_call x1, Pallas kernels, on_device(): pl.pallas_call(functools.partial(kernel, nodes, replicas, chunk), out_sha...  88 us
    unnamed x3, local copies, waits for them, and re-layouts  1.95 us

profile of v8, /device:TPU:0, one launch (start us, length us, event | category | flops | bytes accessed | tf_op | source)
XLA Modules:
  0.0 89.9 jit_solution(17272397545622974438)
XLA Ops:
  0.0 0.0 copy-start
  0.0 0.9 copy-done
  0.9 88.0 %shard_map.37 = f32[128,2560]{1,0:T(8,128)S(1)} custom-call(bf16[256,4096]{1,0:T(8,128)(2,1)} %hidden.1, bf16[256,2560]{1,0:T(8,128)(2,1)} %cotangent.1, f32[20,1024]{1,0:T(8,128)S(1)} %bitcast.1), custom_call_target="tpu_custom_call" | custom-call | flops 5368709120 | bytes 3407872 | tf_op jit(solution)/shard_map/pallas_call | solution.py:395
  88.9 1.1 %copy.5 = f32[128,2560]{1,0:T(8,128)} copy(f32[128,2560]{1,0:T(8,128)S(1)} %shard_map.37) | data formatting | bytes 2621440
Async XLA Ops:
  0.0 0.9 copy-start

commit v9 on v8

--- a/solution.py
+++ b/solution.py
@@ -10,10 +10,10 @@
 
 MESH = pl.DeviceIdType.MESH
 BLOCK = 128
-WINDOW = 4
+WINDOW = 5
 AHEAD = 2
 LATE_HIDDEN = 3
-RELAY_LAG = 2
+RELAY_LAG = 3
 LAST = 2
 
 
@@ -245,10 +245,10 @@
     if square:
         for part in range(len(early)):
             hid_copy(3, part).wait_recv()
-        for j in range(AHEAD):
-            send_cot(j + AHEAD)
-            if j + 1 < AHEAD:
-                pass_on(j + 1)
+        for j in range(1, WINDOW - AHEAD + 1):
+            send_cot(j + AHEAD - 1)
+            if j < AHEAD:
+                pass_on(j)
         for part in range(len(early)):
             turn(3, part)
     else:

time: 90.1 us -> 90.1 us (level)
  no operation moved by 1% of the time
where the time goes in v9:
time: 90.1 us; the launch traced here: 89.9 us
  Pallas kernels  88 us (98%)
  local copies, waits for them, and re-layouts  1.95 us (2%)
    pallas_call x1, Pallas kernels, on_device(): pl.pallas_call(functools.partial(kernel, nodes, replicas, chunk), out_sha...  88 us
    unnamed x3, local copies, waits for them, and re-layouts  1.95 us

profile of v9, /device:TPU:0, one launch (start us, length us, event | category | flops | bytes accessed | tf_op | source)
XLA Modules:
  0.0 89.9 jit_solution(13358221159332526134)
XLA Ops:
  0.0 0.0 copy-start
  0.0 0.9 copy-done
  0.9 88.0 %shard_map.37 = f32[128,2560]{1,0:T(8,128)S(1)} custom-call(bf16[256,4096]{1,0:T(8,128)(2,1)} %hidden.1, bf16[256,2560]{1,0:T(8,128)(2,1)} %cotangent.1, f32[20,1024]{1,0:T(8,128)S(1)} %bitcast.1), custom_call_target="tpu_custom_call" | custom-call | flops 5368709120 | bytes 3407872 | tf_op jit(solution)/shard_map/pallas_call | solution.py:395
  88.9 1.1 %copy.5 = f32[128,2560]{1,0:T(8,128)} copy(f32[128,2560]{1,0:T(8,128)S(1)} %shard_map.37) | data formatting | bytes 2621440
Async XLA Ops:
  0.0 0.9 copy-start

commit v10 on v8

--- a/solution.py
+++ b/solution.py
@@ -286,6 +286,11 @@
 
     def combine(j):
         for part, (first, count) in enumerate(early):
+            if line and part == 1:
+                @pl.when(j >= RELAY_LAG)
+                def _():
+                    relay(j - RELAY_LAG)
+
             pair_copy(j, part).wait_recv()
             for z in range(count):
                 both = levels[j, core, first + z].astype(jnp.float32) + partner_in[j, first + z].astype(jnp.float32)
@@ -329,14 +334,8 @@
             product(j, part)
         combine(j)
 
-        if line:
-            @pl.when(j >= RELAY_LAG)
-            def _():
-                relay(j - RELAY_LAG)
-
     if line:
-        @pl.loop(chunks - RELAY_LAG, chunks)
-        def _(j):
+        for j in range(chunks - RELAY_LAG, chunks - 1):
             relay(j)
 
         for step in range(1, nodes):
@@ -345,6 +344,8 @@
 
         for j in range(chunks):
             product(j, 2)
+
+        relay(chunks - 1)
 
     for group in (range(chunks - LAST), range(chunks - LAST, chunks)):
         for j in group:

time: 90.1 us -> 90.4 us (level)
  no operation moved by 1% of the time
where the time goes in v10:
time: 90.4 us; the launch traced here: 90.2 us
  Pallas kernels  88.3 us (98%)
  local copies, waits for them, and re-layouts  1.95 us (2%)
    pallas_call x1, Pallas kernels, on_device(): pl.pallas_call(functools.partial(kernel, nodes, replicas, chunk), out_sha...  88.3 us
    unnamed x3, local copies, waits for them, and re-layouts  1.95 us

profile of v10, /device:TPU:0, one launch (start us, length us, event | category | flops | bytes accessed | tf_op | source)
XLA Modules:
  0.0 90.2 jit_solution(17083970378145404541)
XLA Ops:
  0.0 0.0 copy-start
  0.0 0.9 copy-done
  0.9 88.3 %shard_map.37 = f32[128,2560]{1,0:T(8,128)S(1)} custom-call(bf16[256,4096]{1,0:T(8,128)(2,1)} %hidden.1, bf16[256,2560]{1,0:T(8,128)(2,1)} %cotangent.1, f32[20,1024]{1,0:T(8,128)S(1)} %bitcast.1), custom_call_target="tpu_custom_call" | custom-call | flops 5368709120 | bytes 3407872 | tf_op jit(solution)/shard_map/pallas_call | solution.py:396
  89.2 1.1 %copy.5 = f32[128,2560]{1,0:T(8,128)} copy(f32[128,2560]{1,0:T(8,128)S(1)} %shard_map.37) | data formatting | bytes 2621440
Async XLA Ops:
  0.0 0.9 copy-start
